TPU v7x, 512 devices: a whole 4x8x8 slice. The times are simulated.
512 devices in a mesh: node: 16 (over x, z_lo), group: 32 (over y, z_hi, core).
Axes of the slice: x: 4, y: 8, z: 8 (z_hi: 2, z_lo: 4; z = z_hi * 4 + z_lo), core: 2. Of those that a mesh axis runs over, the one named last changes fastest.
Arguments:
- queries: bfloat16 [32, 2048, 128], P('group', 'node'), may hold values from -6 to 6
- keys: bfloat16 [32, 2048, 128], P('group', 'node'), may hold values from -6 to 6
- values: bfloat16 [32, 2048, 128], P('group', 'node'), may hold values from -6 to 6
- out_grad: bfloat16 [32, 2048, 12288], P('group', 'node'), may hold values from -6 to 6
- out_weight: bfloat16 [128, 12288], P(None, 'node'), may hold values from -0.0546875 to 0.0546875
- block_offsets: int32 [129], replicated, may hold values from 0 to 1626112, as said below
Outputs:
- bucket: float32 [1638400], P(('node', 'group'))
- qkv_grads: bfloat16 [32, 2048, 384], P('group', 'node')
Inputs may be any that keep to these rules, and one draw needn't show every extreme that they name: block_offsets[b] is a multiple of 128 and block_offsets[b + 1] >= block_offsets[b] + 12288.
All inputs are finite; a program needn't handle non-finite values.
Results may differ from a plain program's by a relative error of at most 0.02.
Values may be sent and summed in bfloat16 or wider, within the bound.
A program may use at most 64 MiB of HBM per device.

v0:
```python
import math

import jax
import jax.numpy as jnp
from jax import lax
from jax.sharding import PartitionSpec as P


def from_behind(block, axis, distance):
    devices = range(lax.axis_size(axis))
    route = [(i - distance, i) for i in devices if i - distance in devices]
    return lax.ppermute(block, axis, route)


def lay_rows(grads_rows, off_rows, flat_rows, per_block):
    below = off_rows[None, :] <= flat_rows[:, None]
    starts = jnp.max(jnp.where(below, off_rows[None, :], -1), axis=1)
    index = jnp.sum(below.astype(jnp.int32), axis=1) - 1
    within = flat_rows - starts
    valid = (index >= 0) & (within < per_block)
    source = jnp.where(valid, index * per_block + within, 0)
    picked = jnp.take(grads_rows, source, axis=0)
    return jnp.where(valid[:, None], picked, jnp.zeros_like(picked))


def per_device(queries, keys, values, out_grad, out_weight, block_offsets):
    query = queries[0]
    own_keys = keys[0]
    own_values = values[0]
    cot = out_grad[0]
    rows = query.shape[0]
    head = query.shape[1]
    width = cot.shape[1]
    scale = 1.0 / math.sqrt(head)
    node_count = lax.axis_size("node")
    group_count = lax.axis_size("group")
    devices = node_count * group_count
    prev_keys, prev_values = from_behind((own_keys, own_values), "node", 1)
    keys_all = jnp.concatenate([prev_keys, own_keys], axis=0)
    values_all = jnp.concatenate([prev_values, own_values], axis=0)
    first = lax.axis_index("node") == 0
    row_pos = jnp.arange(rows)[:, None]
    col_pos = jnp.arange(2 * rows)[None, :]
    allowed = (
        (col_pos > row_pos)
        & (col_pos <= row_pos + rows)
        & ((col_pos >= rows) | jnp.logical_not(first))
    )
    scores = jnp.dot(query, keys_all.T, preferred_element_type=jnp.float32) * scale
    scores = jnp.where(allowed, scores, -jnp.inf)
    top = jnp.max(scores, axis=1, keepdims=True)
    expo = jnp.exp(scores - top)
    probs = expo / jnp.sum(expo, axis=1, keepdims=True)
    probs_low = probs.astype(jnp.bfloat16)
    attended = jnp.dot(probs_low, values_all, preferred_element_type=jnp.float32).astype(
        jnp.bfloat16
    )
    head_grad = jnp.einsum(
        "rd,hd->rh",
        cot,
        lax.all_gather(out_weight, "node", axis=1, tiled=True),
        preferred_element_type=jnp.float32,
    )
    head_low = head_grad.astype(jnp.bfloat16)
    prob_grad = jnp.dot(head_low, values_all.T, preferred_element_type=jnp.float32)
    center = jnp.sum(probs * prob_grad, axis=1, keepdims=True)
    score_grad = (probs * (prob_grad - center) * scale).astype(jnp.bfloat16)
    grad_q = jnp.dot(score_grad, keys_all, preferred_element_type=jnp.float32).astype(jnp.bfloat16)
    keys_grad = jnp.einsum("rc,rh->ch", score_grad, query, preferred_element_type=jnp.float32)
    values_grad = jnp.einsum("rc,rh->ch", probs_low, head_low, preferred_element_type=jnp.float32)
    later_keys, later_values = from_behind((keys_grad[:rows], values_grad[:rows]), "node", -1)
    grad_k = (keys_grad[rows:] + later_keys).astype(jnp.bfloat16)
    grad_v = (values_grad[rows:] + later_values).astype(jnp.bfloat16)
    qkv_grads = jnp.concatenate([grad_q, grad_k, grad_v], axis=1)[None]
    weight_term = jnp.einsum("rh,rd->hd", attended, cot, preferred_element_type=jnp.float32)
    bias_term = jnp.dot(jnp.ones((1, rows), jnp.bfloat16), cot, preferred_element_type=jnp.float32)
    grads = jnp.concatenate([weight_term, bias_term], axis=0)
    blocks = grads.shape[0]
    per_block = width // 128
    grads_rows = grads.reshape(blocks * per_block, 128)
    off_rows = block_offsets // 128
    total_rows = (blocks * per_block + blocks + devices - 1) // devices * devices
    share = total_rows // devices
    flat_rows = jnp.arange(total_rows // node_count * lax.axis_size("node"))
    within_node = lax.psum_scatter(
        lay_rows(grads_rows, off_rows, flat_rows, per_block).astype(jnp.bfloat16),
        "node",
        scatter_dimension=0,
        tiled=True,
    ).astype(jnp.float32)
    summed = lax.psum_scatter(within_node, "group", scatter_dimension=0, tiled=True)
    tokens_all = rows * devices
    bucket = (summed * (1.0 / math.sqrt(tokens_all))).reshape(share * 128)
    return (bucket, qkv_grads)


def solution(mesh):
    return jax.shard_map(
        per_device,
        mesh=mesh,
        in_specs=(
            P("group", "node", None),
            P("group", "node", None),
            P("group", "node", None),
            P("group", "node", None),
            P(None, "node"),
            P(),
        ),
        out_specs=(P(("node", "group")), P("group", "node", None)),
        check_vma=False,
    )
```

profile of v0, /device:TPU:1, one launch (start us, length us, event | category | flops | bytes accessed | tf_op | source)
XLA Modules:
  0.0 346.8 jit_solution(17723106060117462619)
XLA Ops:
  7.3 0.7 all-gather.2.cloned.1.call-update
  8.0 5.6 %collective-permute-start = (bf16[128,128]{1,0:T(8,128)(2,1)}, bf16[128,128]{1,0:T(8,128)(2,1)}, u32[]{:S(2)}, u32[]{:S(2)}) collective-permute-start(bf16[128,128]{1,0:T(8,128)(2,1)} %bitcast.38), channel_id=1, source_target_pairs={{0,32},{32,64},{64,96},{96,128},{128,160},{160,192},{192,224},{224... | collective-permute-start | bytes 98312 | tf_op jit(solution)/shard_map/ppermute | solution.py:12
  13.6 3.4 collective-permute-start.1
  17.0 0.7 and_select_fusion.1
  18.2 1.9 select_reduce_fusion
  20.5 1.0 fusion.38
  21.6 2.9 fusion.5
  24.5 4.0 %pad_maximum_fusion = bf16[129,12288]{1,0:T(8,128)(2,1)} fusion(bf16[1,12288]{1,0:T(2,128)(2,1)S(1)} %fusion.3, bf16[128,12288]{1,0:T(8,128)(2,1)} %fusion.5), kind=kLoop, calls=%fused_computation.4 | loop fusion | flops 6340608 | bytes 6340608 | tf_op jit(solution)/shard_map/concatenate | solution.py:77
  28.4 5.8 %reshape.92 = bf16[12384,128]{1,0:T(8,128)(2,1)} reshape(bf16[129,12288]{1,0:T(8,128)(2,1)} %pad_maximum_fusion) | data formatting | bytes 6340608 | tf_op jit(solution)/shard_map/reshape | solution.py:80
  34.2 26.6 %gather_fusion = bf16[12800,128]{1,0:T(8,128)(2,1)} fusion(bf16[12384,128]{1,0:T(8,128)(2,1)} %reshape.92, s32[13312]{0:T(1024)S(1)} %pad_clamp_fusion), kind=kCustom, calls=%fused_computation | custom fusion | bytes 6604800 | tf_op jit(solution)/shard_map/jit(_take)/gather | solution.py:22
  60.8 10.9 %select_convert_fusion = bf16[12800,128]{1,0:T(8,128)(2,1)} fusion(bf16[12800,128]{1,0:T(8,128)(2,1)} %gather_fusion, pred[12800]{0:T(1024)(128)(4,1)S(1)} %compare_and_fusion, pred[12800]{0:T(1024)(128)(4,1)S(1)} %get-tuple-element.12), kind=kLoop, calls=%fused_computation.5 | loop fusion | flops 3276800 | bytes 6579200 | tf_op jit(solution)/shard_map/convert_element_type | solution.py:86
  71.7 1.3 dynamic-slice.4
  73.6 30.1 %all-gather.2.cloned.1.call-done = bf16[128,12288]{1,0:T(8,128)(2,1)} async-done(((bf16[128,768]{1,0:T(8,128)(2,1)}), bf16[128,12288]{1,0:T(8,128)(2,1)}) %all-gather.2.cloned.1.call-update) | async-done | bytes 3145744 | tf_op jit(solution)/shard_map/all_gather | solution.py:61
  103.7 2.9 fusion.9
  106.8 1.3 collective-permute-start.3
  109.9 1.3 collective-permute-start.2
  111.2 1.6 convolution_convert_fusion
  113.4 88.2 %reduce-scatter.4.cloned.1.call-done = bf16[800,128]{1,0:T(8,128)(2,1)} async-done(((bf16[12800,128]{1,0:T(8,128)(2,1)}), bf16[800,128]{1,0:T(8,128)(2,1)}) %reduce-scatter.4.cloned.1.call-update) | async-done | bytes 204816 | tf_op jit(solution)/shard_map/reduce_scatter | solution.py:85
  201.6 1.0 convert_element_type.34
  202.6 97.4 %fusion = f32[32,128]{1,0:T(8,128)} fusion(f32[800,128]{1,0:T(8,128)S(1)} %convert_element_type.34), kind=kCustom, calls=%all-reduce-scatter | all-reduce-scatter fusion | flops 131073 | bytes 428032
  300.0 0.7 slice.22
  300.7 1.3 collective-permute-start.9
  302.0 7.7 %collective-permute-start.10 = (f32[25,128]{1,0:T(8,128)S(1)}, f32[25,128]{1,0:T(8,128)S(1)}, u32[]{:S(2)}, u32[]{:S(2)}) collective-permute-start(f32[25,128]{1,0:T(8,128)S(1)} %slice.22), channel_id=1, source_target_pairs={{0,7},{1,8},{2,9},{3,10},{4,11},{5,12},{6,13},{7,14},{8,15},{9,16}... | collective-permute-start | bytes 38408
  309.7 0.9 fusion.17
  310.6 4.3 %collective-permute-start.8 = (f32[32,128]{1,0:T(8,128)}, f32[32,128]{1,0:T(8,128)S(1)}, u32[]{:S(2)}, u32[]{:S(2)}) collective-permute-start(f32[32,128]{1,0:T(8,128)} %fusion), channel_id=1, source_target_pairs={{0,5},{1,6},{2,7},{3,8},{4,9},{5,10},{6,11},{7,12},{8,13},{9,14},{... | collective-permute-start | bytes 49160
  314.9 9.8 %collective-permute-start.7 = (f32[32,128]{1,0:T(8,128)}, f32[32,128]{1,0:T(8,128)S(1)}, u32[]{:S(2)}, u32[]{:S(2)}) collective-permute-start(f32[32,128]{1,0:T(8,128)} %fusion), channel_id=1, source_target_pairs={{0,4},{1,5},{2,6},{3,7},{4,8},{5,9},{6,10},{7,11},{8,12},{9,13},{1... | collective-permute-start | bytes 49160
  324.7 1.3 collective-permute-start.6
  326.0 3.1 collective-permute-start.5
  329.2 7.0 %collective-permute-start.4 = (f32[32,128]{1,0:T(8,128)}, f32[32,128]{1,0:T(8,128)S(1)}, u32[]{:S(2)}, u32[]{:S(2)}) collective-permute-start(f32[32,128]{1,0:T(8,128)} %fusion), channel_id=1, source_target_pairs={{0,1},{1,2},{2,3},{3,4},{4,5},{5,6},{6,7},{7,8},{8,9},{9,10},{10,1... | collective-permute-start | bytes 49160
  336.2 0.8 maximum_bitcast_fusion
  337.0 0.8 copy.19
  337.7 1.6 concatenate.16
  (41 shorter events, 4.3 us)
Async XLA Ops:
  7.2 10.5 %copy-start = (bf16[1,128,12288]{2,1,0:T(8,128)(2,1)S(1)}, bf16[1,128,12288]{2,1,0:T(8,128)(2,1)}, u32[]{:S(2)}) copy-start(bf16[1,128,12288]{2,1,0:T(8,128)(2,1)} %param.9) | copy-start | bytes 9437188
  7.2 13.3 %copy-start.4 = (bf16[1,128,128]{2,1,0:T(8,128)(2,1)S(1)}, bf16[1,128,128]{2,1,0:T(8,128)(2,1)}, u32[]{:S(2)}) copy-start(bf16[1,128,128]{2,1,0:T(8,128)(2,1)} %param.7) | copy-start | bytes 98308
  7.2 14.4 %copy-start.2 = (bf16[1,128,128]{2,1,0:T(8,128)(2,1)S(1)}, bf16[1,128,128]{2,1,0:T(8,128)(2,1)}, u32[]{:S(2)}) copy-start(bf16[1,128,128]{2,1,0:T(8,128)(2,1)} %param.8) | copy-start | bytes 98308
  7.2 13.3 %copy-start.3 = (bf16[1,128,128]{2,1,0:T(8,128)(2,1)S(1)}, bf16[1,128,128]{2,1,0:T(8,128)(2,1)}, u32[]{:S(2)}) copy-start(bf16[1,128,128]{2,1,0:T(8,128)(2,1)} %param.6) | copy-start | bytes 98308
  7.2 96.5 %all-gather.2.cloned.1.call-start = ((), (), s32[]{:S(2)}) async-start(), calls=%async_computation.2 | async-start | bytes 3342336 | tf_op jit(solution)/shard_map/all_gather | solution.py:61
  7.9 193.7 %reduce-scatter.4.cloned.1.call-start = ((), (), s32[]{:S(2)}) async-start(), calls=%async_computation.1 | async-start | bytes 3481600 | tf_op jit(solution)/shard_map/reduce_scatter | solution.py:85
  8.0 12.5 %collective-permute-start = (bf16[128,128]{1,0:T(8,128)(2,1)}, bf16[128,128]{1,0:T(8,128)(2,1)}, u32[]{:S(2)}, u32[]{:S(2)}) collective-permute-start(bf16[128,128]{1,0:T(8,128)(2,1)} %bitcast.38), channel_id=1, source_target_pairs={{0,32},{32,64},{64,96},{96,128},{128,160},{160,192},{192,224},{224... | collective-permute-start | bytes 98312 | tf_op jit(solution)/shard_map/ppermute | solution.py:12
  13.6 8.0 %collective-permute-start.1 = (bf16[128,128]{1,0:T(8,128)(2,1)}, bf16[128,128]{1,0:T(8,128)(2,1)S(1)}, u32[]{:S(2)}, u32[]{:S(2)}) collective-permute-start(bf16[128,128]{1,0:T(8,128)(2,1)} %bitcast.35), channel_id=1, source_target_pairs={{0,32},{32,64},{64,96},{96,128},{128,160},{160,192},{192,224},{224... | collective-permute-start | bytes 98312 | tf_op jit(solution)/shard_map/ppermute | solution.py:12
  106.8 5.9 %collective-permute-start.3 = (f32[128,128]{0,1:T(8,128)S(1)}, f32[128,128]{0,1:T(8,128)S(1)}, u32[]{:S(2)}, u32[]{:S(2)}) collective-permute-start(f32[128,128]{0,1:T(8,128)S(1)} %slice.21), channel_id=1, source_target_pairs={{32,0},{64,32},{96,64},{128,96},{160,128},{192,160},{224,192},{256... | collective-permute-start | bytes 196616 | tf_op jit(solution)/shard_map/ppermute | solution.py:12
  108.6 0.7 copy-start.1
  109.9 199.8 %collective-permute-start.2 = (f32[128,128]{0,1:T(8,128)}, f32[128,128]{0,1:T(8,128)}, u32[]{:S(2)}, u32[]{:S(2)}) collective-permute-start(f32[128,128]{0,1:T(8,128)} %slice.19), channel_id=1, source_target_pairs={{32,0},{64,32},{96,64},{128,96},{160,128},{192,160},{224,192},{256... | collective-permute-start | bytes 196616 | tf_op jit(solution)/shard_map/ppermute | solution.py:12
  300.7 28.5 %collective-permute-start.9 = (f32[32,128]{1,0:T(8,128)}, f32[32,128]{1,0:T(8,128)S(1)}, u32[]{:S(2)}, u32[]{:S(2)}) collective-permute-start(f32[32,128]{1,0:T(8,128)} %fusion), channel_id=1, source_target_pairs={{0,6},{1,7},{2,8},{3,9},{4,10},{5,11},{6,12},{7,13},{8,14},{9,15},... | collective-permute-start | bytes 49160
  302.0 24.1 %collective-permute-start.10 = (f32[25,128]{1,0:T(8,128)S(1)}, f32[25,128]{1,0:T(8,128)S(1)}, u32[]{:S(2)}, u32[]{:S(2)}) collective-permute-start(f32[25,128]{1,0:T(8,128)S(1)} %slice.22), channel_id=1, source_target_pairs={{0,7},{1,8},{2,9},{3,10},{4,11},{5,12},{6,13},{7,14},{8,15},{9,16}... | collective-permute-start | bytes 38408
  310.6 27.2 %collective-permute-start.8 = (f32[32,128]{1,0:T(8,128)}, f32[32,128]{1,0:T(8,128)S(1)}, u32[]{:S(2)}, u32[]{:S(2)}) collective-permute-start(f32[32,128]{1,0:T(8,128)} %fusion), channel_id=1, source_target_pairs={{0,5},{1,6},{2,7},{3,8},{4,9},{5,10},{6,11},{7,12},{8,13},{9,14},{... | collective-permute-start | bytes 49160
  314.9 22.8 %collective-permute-start.7 = (f32[32,128]{1,0:T(8,128)}, f32[32,128]{1,0:T(8,128)S(1)}, u32[]{:S(2)}, u32[]{:S(2)}) collective-permute-start(f32[32,128]{1,0:T(8,128)} %fusion), channel_id=1, source_target_pairs={{0,4},{1,5},{2,6},{3,7},{4,8},{5,9},{6,10},{7,11},{8,12},{9,13},{1... | collective-permute-start | bytes 49160
  324.7 13.0 %collective-permute-start.6 = (f32[32,128]{1,0:T(8,128)}, f32[32,128]{1,0:T(8,128)S(1)}, u32[]{:S(2)}, u32[]{:S(2)}) collective-permute-start(f32[32,128]{1,0:T(8,128)} %fusion), channel_id=1, source_target_pairs={{0,3},{1,4},{2,5},{3,6},{4,7},{5,8},{6,9},{7,10},{8,11},{9,12},{10... | collective-permute-start | bytes 49160
  326.0 11.7 %collective-permute-start.5 = (f32[32,128]{1,0:T(8,128)}, f32[32,128]{1,0:T(8,128)S(1)}, u32[]{:S(2)}, u32[]{:S(2)}) collective-permute-start(f32[32,128]{1,0:T(8,128)} %fusion), channel_id=1, source_target_pairs={{0,2},{1,3},{2,4},{3,5},{4,6},{5,7},{6,8},{7,9},{8,10},{9,11},{10,... | collective-permute-start | bytes 49160
  329.2 8.6 %collective-permute-start.4 = (f32[32,128]{1,0:T(8,128)}, f32[32,128]{1,0:T(8,128)S(1)}, u32[]{:S(2)}, u32[]{:S(2)}) collective-permute-start(f32[32,128]{1,0:T(8,128)} %fusion), channel_id=1, source_target_pairs={{0,1},{1,2},{2,3},{3,4},{4,5},{5,6},{6,7},{7,8},{8,9},{9,10},{10,1... | collective-permute-start | bytes 49160
Sparse Core Ops, SparseCore 0:
  10.1 93.5 all-gather.1
  106.6 95.0 reduce-scatter.3
where the time goes:
time: 351 us; the launch traced here: 347 us
  waiting for transfers between devices  119 us (34%)
  blocking collectives  97.4 us (28%)
  starting transfers between devices  46.1 us (13%)
  local copies, waits for them, and re-layouts  38 us (11%)
  other arithmetic  21.7 us (6%)
  between operations  15 us (4%)
  matrix products  9.47 us (3%)
    unnamed x1, blocking collectives  97.4 us
    reduce_scatter x1, waiting for transfers between devices, per_device(): lax.psum_scatter(lay_rows(grads_rows, off_rows, flat_rows, per_block).ast...  88.2 us
    unnamed x7, starting transfers between devices  34.5 us
    all_gather x1, waiting for transfers between devices, per_device(): lax.all_gather(out_weight, 'node', axis=1, tiled=True)  30.1 us
    gather x1, local copies, waits for them, and re-layouts, lay_rows(): picked = jnp.take(grads_rows, source, axis=0)  26.6 us
    ppermute x4, starting transfers between devices, from_behind(): return lax.ppermute(block, axis, route)  11.5 us
    convert_element_type x1, other arithmetic, per_device(): lay_rows(grads_rows, off_rows, flat_rows, per_block).astype(jnp.bfloat16)  10.9 us
  transfers between devices with their start and end apart: 13, of which 2 were waited for; matrix products, arithmetic and copies ran while one was open for 47% of the time, Pallas kernels for 0%

commit v1 on v0

v1 whole, which is shorter than its diff:
```python
import math

import jax
import jax.numpy as jnp
from jax import lax
from jax.experimental import pallas as pl
from jax.experimental.pallas import tpu as pltpu
from jax.sharding import PartitionSpec as P

MESH = pl.DeviceIdType.MESH
BF = jnp.bfloat16
F32 = jnp.float32

HEAD = 128
TOK = 128
WIDTH = 12288
COLS = 768
PER = 96
NB = 80
B0 = 56
PAD = 56
GROWS = PAD + NB * PER + PAD
WIN = 50
CHUNK = 400
HALVES = ((0, 208), (208, 192))
OCH = 6
OW = WIDTH // OCH

CHAINS = ((-1, 0, 4), (1, 1, 4), (-1, 1, 3), (1, 0, 3))


def dot(a, b, ca, cb):
    return lax.dot_general(a, b, (((ca,), (cb,)), ((), ())), preferred_element_type=F32)


def kernel(q_hbm, k_hbm, v_hbm, o_hbm, w_hbm, off, bucket, qkv,
           O, W, G, F, S, R, At, q, K, V, probs, hg, gsend, grecv, send2, recv2, tab,
           lsem, ssem, rsem, s2send, s2recv):
    node = lax.axis_index("node")
    group = lax.axis_index("group")
    x, zlo = node // 4, node % 4
    y, zhi, k = group // 4, (group % 4) // 2, group % 2
    z = zhi * 4 + zlo

    def did(dx, dy, dz, dc):
        dx, dy, dz = lax.rem(dx + 8, 4), lax.rem(dy + 16, 8), lax.rem(dz + 16, 8)
        return (dx * 4 + lax.rem(dz, 4), dy * 4 + dz // 4 * 2 + dc)

    sib = did(x, y, z, 1 - k)
    nxt = (lax.rem(node + 1, 16), group)
    prv = (lax.rem(node + 15, 16), group)
    counter = [0]

    def send(src, dst, dev):
        i = counter[0]
        counter[0] += 1
        cp = pltpu.make_async_remote_copy(
            src_ref=src, dst_ref=dst, send_sem=ssem.at[i], recv_sem=rsem.at[i],
            device_id=dev, device_id_type=MESH)
        cp.start()
        sent.append(cp)
        return cp

    sent = []

    own_rows = pl.ds(pl.multiple_of(TOK * k, TOK), TOK)
    locals_ = [
        pltpu.make_async_copy(q_hbm.at[0], q, lsem.at[0]),
        pltpu.make_async_copy(k_hbm.at[0], K.at[pl.ds(TOK, TOK)], lsem.at[1]),
        pltpu.make_async_copy(v_hbm.at[0], V.at[pl.ds(TOK, TOK)], lsem.at[2]),
        pltpu.make_async_copy(o_hbm.at[0], O.at[own_rows], lsem.at[3]),
        pltpu.make_async_copy(w_hbm, W.at[node], lsem.at[4]),
    ]
    for c in locals_:
        c.start()

    bar = pltpu.get_barrier_semaphore()

    def sig(dev):
        pl.semaphore_signal(bar, inc=1, device_id=dev, device_id_type=MESH)

    near = [sib, nxt, prv, did(x, y + 1, z, k), did(x, y - 1, z, k), did(x, y, z + 1, k),
            did(x, y, z - 1, k), did(x + 1, y, z, k), did(x - 1, y, z, k)]
    for dev in near:
        sig(dev)
    src_core = x // 2
    odd = lax.rem(x, 2)
    mine = src_core == k

    def sig_far(i, carry):
        sx, r = i // 8, lax.rem(i, 8)
        sy = jnp.where(odd == 1, r, y)
        sz = jnp.where(odd == 1, z, r)

        @pl.when(jnp.logical_not(mine & (sx == x) & (sy == y) & (sz == z)))
        def _():
            sig(did(sx, sy, sz, src_core))
        return carry
    lax.fori_loop(0, 32, sig_far, 0)

    b0 = B0 * k

    def off_row(i):
        return lax.shift_right_logical(off[jnp.clip(i, 0, 128)], 7)

    def advance(i, f0):
        step = (i + 1 <= 128) & (off_row(i + 1) <= f0)
        return i + step.astype(jnp.int32)

    first = jnp.where(k == 0, -1, 61)
    flat0 = 6400 * k
    first = lax.fori_loop(0, 5, lambda _, i: advance(i, flat0), first)

    def table(w, i):
        f0 = flat0 + WIN * w
        i = advance(i, f0)
        a, b = off_row(i), off_row(i + 1)
        one = PAD + (i - b0) * PER + jnp.clip(f0 - a, 0, PER)
        two = PAD + (jnp.minimum(i + 1, 128) - b0) * PER + jnp.clip(f0 - b, -PAD, 0)
        tab[0, w] = jnp.clip(one, 0, GROWS - 56)
        tab[1, w] = jnp.clip(two, 0, GROWS - 56)
        tab[2, w] = jnp.where(i < 0, 0, a + PER - f0)
        tab[3, w] = jnp.where(i + 1 > 128, 2 * WIN, b - f0)
        return i
    lax.fori_loop(0, 128, table, first)

    rows8 = lax.broadcasted_iota(jnp.int32, (8, 2 * TOK), 0)
    At[pl.ds(HEAD, 8), :] = jnp.where(rows8 == 0, 1.0, 0.0)

    pl.semaphore_wait(bar, len(near) + 32 - mine.astype(jnp.int32))

    cp_k = send(k_hbm.at[0], K.at[pl.ds(0, TOK)], nxt)
    cp_v = send(v_hbm.at[0], V.at[pl.ds(0, TOK)], nxt)

    half = pl.multiple_of(64 * k, 64)

    def nbr(axis, delta):
        along_z = (k == 0) if axis == 0 else (k == 1)
        return did(x + jnp.where(along_z, 0, delta), y, z + jnp.where(along_z, delta, 0), k)

    def nid(a, b):
        dx, dz = jnp.where(k == 0, b, a), jnp.where(k == 0, a, b)
        return lax.rem(x + dx + 4, 4) * 4 + lax.rem(zlo + dz + 4, 4)

    def wpart(n, sub=None):
        if sub is None:
            return W.at[n, pl.ds(half, 64)]
        return W.at[n, pl.ds(half + 32 * sub, 32)]

    w_own = w_hbm.at[pl.ds(half, 64)]
    m1 = {d: send(w_own, wpart(node), nbr(0, d)) for d in (1, -1)}
    m2 = {}
    for d in (1, -1):
        m2[0, d] = send(w_own, wpart(node), nbr(1, d))
    cp_o = [send(o_hbm.at[0, :, pl.ds(OW * j, OW)], O.at[own_rows, pl.ds(OW * j, OW)], sib)
            for j in range(OCH)]

    f1, f2, wsib = {}, {}, []

    def stage1(d):
        m1[d].wait_recv()
        n = nid(-d, 0)
        f1[d] = send(wpart(n, 0 if d == 1 else 1), wpart(n, 0 if d == 1 else 1), nbr(0, d))
        for e in (1, -1):
            m2[-d, e] = send(wpart(n), wpart(n), nbr(1, e))
        wsib.append(send(wpart(n), wpart(n), sib))

    def stage1_far():
        for d in (1, -1):
            f1[d].wait_recv()
        n = nid(2, 0)
        for e in (1, -1):
            m2[2, e] = send(wpart(n), wpart(n), nbr(1, e))
        wsib.append(send(wpart(n), wpart(n), sib))

    def stage2(a):
        for e in (1, -1):
            m2[a, e].wait_recv()
            n = nid(a, -e)
            sub = 0 if e == 1 else 1
            f2[a, e] = send(wpart(n, sub), wpart(n, sub), nbr(1, e))
            wsib.append(send(wpart(n), wpart(n), sib))

    def stage2_far(a):
        for e in (1, -1):
            f2[a, e].wait_recv()
        n = nid(a, 2)
        wsib.append(send(wpart(n), wpart(n), sib))

    stage1(1)
    stage1(-1)

    for c in locals_[:3]:
        c.wait()
    cp_k.wait_recv()
    cp_v.wait_recv()
    scale = 1.0 / math.sqrt(HEAD)
    scores = dot(q[...], K[...], 1, 1) * scale
    rp = lax.broadcasted_iota(jnp.int32, (TOK, 2 * TOK), 0)
    cpos = lax.broadcasted_iota(jnp.int32, (TOK, 2 * TOK), 1)
    lowest = jnp.where(node == 0, TOK, 0)
    allowed = (cpos > rp) & (cpos <= rp + TOK) & (cpos >= lowest)
    scores = jnp.where(allowed, scores, -jnp.inf)
    top = jnp.max(scores, axis=1, keepdims=True)
    expo = jnp.exp(scores - top)
    pr = expo / jnp.sum(expo, axis=1, keepdims=True)
    probs[...] = pr
    att = dot(pr.astype(BF), V[...], 1, 0)
    att_cols = pl.ds(pl.multiple_of(TOK * k, TOK), TOK)
    At[pl.ds(0, HEAD), att_cols] = jnp.transpose(att)
    cp_a = send(At.at[pl.ds(0, HEAD), att_cols], At.at[pl.ds(0, HEAD), att_cols], sib)

    stage1_far()
    stage2(0)

    cp_a.wait_recv()
    locals_[3].wait()
    lhs = At[pl.ds(pl.multiple_of(b0, 8), NB), :].astype(BF)
    for j in range(OCH):
        cp_o[j].wait_recv()

        def mul(t, carry):
            prod = dot(lhs, O[:, pl.ds(pl.multiple_of(256 * t, 256), 256)], 1, 0)
            G[pl.ds(PAD + 2 * t, NB, stride=PER), :] = prod[:, :128]
            G[pl.ds(PAD + 2 * t + 1, NB, stride=PER), :] = prod[:, 128:]
            return carry
        lax.fori_loop(j * (OW // 256), (j + 1) * (OW // 256), mul, 0)

    rwin = lax.broadcasted_iota(jnp.int32, (56, 128), 0)

    def gather(delta):
        for a, p in ((0, y), (1, z)):
            d = lax.rem(p + delta + 16, 8)
            for m in range(8):
                if a == 0:
                    w = 16 * (m % 4) + 2 * d + m // 4
                else:
                    w = 64 + 16 * lax.rem(d, 4) + 2 * m + d // 4
                one = G[pl.ds(tab[0, w], 56), :]
                two = G[pl.ds(tab[1, w], 56), :]
                F[a, pl.ds(WIN * m, 56), :] = jnp.where(
                    rwin < tab[2, w], one, jnp.where(rwin >= tab[3, w], two, 0.0))
            S[a, d] = F[a, pl.ds(0, CHUNK), :].astype(BF)

    msgs = {}

    def ring(ch, s):
        direction, h, n = CHAINS[ch]
        lo, size = HALVES[h]
        rows = pl.ds(lo, size)
        for a, p in ((0, y), (1, z)):
            d = lax.rem(p + direction * (n - s) + 16, 8)
            if s > 0:
                msgs[a, ch, s - 1].wait_recv()
                S[a, d, rows] = (S[a, d, rows].astype(F32)
                                 + R[a, ch, s - 1, pl.ds(0, size)].astype(F32)).astype(BF)
            to = did(x, y + direction, z, k) if a == 0 else did(x, y, z + direction, k)
            msgs[a, ch, s] = send(S.at[a, d, rows], R.at[a, ch, s, pl.ds(0, size)], to)

    gather(4)
    ring(0, 0)
    ring(1, 0)
    gather(-3)
    ring(2, 0)
    gather(3)
    ring(3, 0)
    gather(-2)
    gather(2)
    for ch in range(4):
        ring(ch, 1)
    stage2(-1)
    stage2(1)
    stage2_far(0)
    gather(-1)
    gather(1)
    for ch in range(4):
        ring(ch, 2)
    gather(0)
    stage2(2)
    stage2_far(-1)
    stage2_far(1)
    for ch in range(2):
        ring(ch, 3)
    stage2_far(2)

    locals_[4].wait()
    for c in wsib:
        c.wait_recv()
    hg[...] = jnp.zeros((TOK, HEAD), F32)

    def head(n, carry):
        cols = pl.ds(pl.multiple_of(COLS * n, COLS), COLS)
        hg[...] += dot(O[own_rows, cols], W[n], 1, 1)
        return carry
    lax.fori_loop(0, 16, head, 0)
    head_low = hg[...].astype(BF)
    prob_grad = dot(head_low, V[...], 1, 1)
    pr = probs[...]
    center = jnp.sum(pr * prob_grad, axis=1, keepdims=True)
    sg = pr * (prob_grad - center) * scale
    grad_q = dot(sg.astype(BF), K[...], 1, 0)
    kg = dot(jnp.transpose(sg).astype(BF), q[...], 1, 0)
    vg = dot(jnp.transpose(pr).astype(BF), head_low, 1, 0)
    gsend[pl.ds(0, TOK), :] = kg[:TOK].astype(BF)
    gsend[pl.ds(TOK, TOK), :] = vg[:TOK].astype(BF)
    cp_g = send(gsend, grecv, prv)
    qkv[0, :, pl.ds(0, HEAD)] = grad_q.astype(BF)
    hg[...] = kg[TOK:]
    probs[:, pl.ds(0, HEAD)] = vg[TOK:]

    last = {0: (0, 3), 1: (3, 2), 2: (2, 2), 3: (1, 3)}
    for a, p in ((0, y), (1, z)):
        for h, (lo, size) in enumerate(HALVES):
            total = S[a, p, pl.ds(lo, size)].astype(F32)
            for ch, (direction, hh, n) in enumerate(CHAINS):
                if hh == h:
                    msgs[a, ch, n - 1].wait_recv()
                    total = total + R[a, ch, n - 1, pl.ds(0, size)].astype(F32)
            F[a, pl.ds(lo, size), :] = total
        for i in range(16):
            send2[16 * a + i] = F[a, pl.ds(25 * i, 32), :].astype(BF)

        def scatter(i, carry):
            r, dc = i // 2, lax.rem(i, 2)
            dx = 2 * k + a
            dy = y if a == 0 else r
            dz = r if a == 0 else z
            slot = x * 8 + (z if a == 0 else y)
            here = (dx == x) & (dy == y) & (dz == z) & (dc == k)

            @pl.when(here)
            def _():
                pltpu.make_async_copy(send2.at[16 * a + i], recv2.at[slot], s2recv).start()

            @pl.when(jnp.logical_not(here))
            def _():
                pltpu.make_async_remote_copy(
                    src_ref=send2.at[16 * a + i], dst_ref=recv2.at[slot],
                    send_sem=s2send, recv_sem=s2recv,
                    device_id=did(dx, dy, dz, dc), device_id_type=MESH).start()
            return carry
        lax.fori_loop(0, 16, scatter, 0)

    cp_g.wait_recv()
    qkv[0, :, pl.ds(HEAD, HEAD)] = (hg[...] + grecv[pl.ds(0, TOK), :].astype(F32)).astype(BF)
    qkv[0, :, pl.ds(2 * HEAD, HEAD)] = (
        probs[:, pl.ds(0, HEAD)] + grecv[pl.ds(TOK, TOK), :].astype(F32)).astype(BF)

    pltpu.make_async_remote_copy(
        src_ref=send2, dst_ref=recv2, send_sem=s2send, recv_sem=s2recv,
        device_id=sib, device_id_type=MESH).wait_recv()
    acc = recv2[0].astype(F32)
    for s in range(1, 32):
        acc = acc + recv2[s].astype(F32)
    bucket[...] = acc[:25] * (1.0 / math.sqrt(65536))

    for c in sent:
        c.wait_send()

    def drain(count):
        pltpu.make_async_remote_copy(
            src_ref=send2.at[pl.ds(0, count)], dst_ref=recv2.at[pl.ds(0, count)],
            send_sem=s2send, recv_sem=s2recv, device_id=sib, device_id_type=MESH).wait_send()

    @pl.when(mine)
    def _():
        drain(31)

    @pl.when(jnp.logical_not(mine))
    def _():
        drain(32)


def per_device(queries, keys, values, out_grad, out_weight, block_offsets):
    hbm = pl.BlockSpec(memory_space=pl.ANY)
    vmem = pl.BlockSpec(memory_space=pltpu.VMEM)
    messages = 96
    bucket, qkv = pl.pallas_call(
        kernel,
        out_shape=(jax.ShapeDtypeStruct((25, 128), F32), jax.ShapeDtypeStruct((1, TOK, 3 * HEAD), BF)),
        in_specs=[hbm] * 5 + [pl.BlockSpec(memory_space=pltpu.SMEM)],
        out_specs=(vmem, vmem),
        scratch_shapes=[
            pltpu.VMEM((2 * TOK, WIDTH), BF),
            pltpu.VMEM((16, HEAD, COLS), BF),
            pltpu.VMEM((GROWS, 128), F32),
            pltpu.VMEM((2, 408, 128), F32),
            pltpu.VMEM((2, 8, CHUNK, 128), BF),
            pltpu.VMEM((2, 4, 4, 208, 128), BF),
            pltpu.VMEM((HEAD + 8, 2 * TOK), F32),
            pltpu.VMEM((TOK, HEAD), BF),
            pltpu.VMEM((2 * TOK, HEAD), BF),
            pltpu.VMEM((2 * TOK, HEAD), BF),
            pltpu.VMEM((TOK, 2 * TOK), F32),
            pltpu.VMEM((TOK, HEAD), F32),
            pltpu.VMEM((2 * TOK, HEAD), BF),
            pltpu.VMEM((2 * TOK, HEAD), BF),
            pltpu.VMEM((32, 32, 128), BF),
            pltpu.VMEM((32, 32, 128), BF),
            pltpu.SMEM((4, 128), jnp.int32),
            pltpu.SemaphoreType.DMA((5,)),
            pltpu.SemaphoreType.DMA((messages,)),
            pltpu.SemaphoreType.DMA((messages,)),
            pltpu.SemaphoreType.DMA,
            pltpu.SemaphoreType.DMA,
        ],
        compiler_params=pltpu.CompilerParams(
            collective_id=0, has_side_effects=True, vmem_limit_bytes=40 << 20),
        name="attention_backward",
    )(queries, keys, values, out_grad, out_weight, block_offsets)
    return bucket.reshape(3200), qkv


def solution(mesh):
    return jax.shard_map(
        per_device,
        mesh=mesh,
        in_specs=(
            P("group", "node", None),
            P("group", "node", None),
            P("group", "node", None),
            P("group", "node", None),
            P(None, "node"),
            P(),
        ),
        out_specs=(P(("node", "group")), P("group", "node", None)),
        check_vma=False,
    )
```

time: 351 us -> 71.8 us (0.20); the launches traced: 347 us -> 71.2 us
  waiting for transfers between devices: 119 us -> 0 us
  blocking collectives: 97.4 us -> 0 us
  Pallas kernels: 0 us -> 63.5 us
  starting transfers between devices: 46.1 us -> 0 us
  local copies, waits for them, and re-layouts: 38 us -> 7.01 us
  other arithmetic: 21.7 us -> 0 us
  between operations: 15 us -> 0.65 us
  matrix products: 9.47 us -> 0 us
    unnamed x1 -> x0, blocking collectives: 97.4 us -> none
    reduce_scatter x1 -> x0, waiting for transfers between devices: 88.2 us -> none  [per_device(): lax.psum_scatter(lay_rows(grads_rows, off_rows, flat_rows, per_block).ast...]
    pallas_call x0 -> x1, Pallas kernels: none -> 63.5 us  [per_device(): pl.pallas_call(kernel, out_shape=(jax.ShapeDtypeStruct((25, 128), F32), j...]
    unnamed x7 -> x0, starting transfers between devices: 34.5 us -> none
    all_gather x1 -> x0, waiting for transfers between devices: 30.1 us -> none  [per_device(): lax.all_gather(out_weight, 'node', axis=1, tiled=True)]
    gather x1 -> x0, local copies, waits for them, and re-layouts: 26.6 us -> none  [lay_rows(): picked = jnp.take(grads_rows, source, axis=0)]
    convert_element_type x5 -> x0, other arithmetic: 13.4 us -> none  [the longest x1 10.9 us: per_device(): lay_rows(grads_rows, off_rows, flat_rows, per_block).astype(jnp.bfloat16)]
    ppermute x4 -> x0, starting transfers between devices: 11.5 us -> none  [from_behind(): return lax.ppermute(block, axis, route)]
  transfers between devices with their start and end apart: 13 -> 0, of which waited for: 2 -> 0; matrix products, arithmetic and copies ran while one was open for 47% -> 0% of each run, Pallas kernels for 0% -> 0%
where the time goes in v1:
time: 71.8 us; the launch traced here: 71.2 us
  Pallas kernels  63.5 us (88%)
  local copies, waits for them, and re-layouts  7.01 us (10%)
    pallas_call x1, Pallas kernels, per_device(): pl.pallas_call(kernel, out_shape=(jax.ShapeDtypeStruct((25, 128), F32), j...  63.5 us
    unnamed x14, local copies, waits for them, and re-layouts  7.01 us

profile of v1, /device:TPU:1, one launch (start us, length us, event | category | flops | bytes accessed | tf_op | source)
XLA Modules:
  0.0 71.2 jit_solution(9126699086776065347)
XLA Ops:
  0.6 0.0 copy-start
  0.6 1.9 %copy-done = bf16[1,128,12288]{2,1,0:T(8,128)(2,1)S(1)} copy-done((bf16[1,128,12288]{2,1,0:T(8,128)(2,1)S(1)}, bf16[1,128,12288]{2,1,0:T(8,128)(2,1)}, u32[]{:S(2)}) %copy-start) | copy-done | bytes 3145752
  2.5 0.0 copy-start.1
  2.5 0.9 %copy-done.1 = bf16[128,768]{1,0:T(8,128)(2,1)S(1)} copy-done((bf16[128,768]{1,0:T(8,128)(2,1)S(1)}, bf16[128,768]{1,0:T(8,128)(2,1)}, u32[]{:S(2)}) %copy-start.1) | copy-done | bytes 196632
  3.4 0.0 copy-start.2
  3.5 0.8 %copy-done.2 = bf16[1,128,128]{2,1,0:T(8,128)(2,1)S(1)} copy-done((bf16[1,128,128]{2,1,0:T(8,128)(2,1)S(1)}, bf16[1,128,128]{2,1,0:T(8,128)(2,1)}, u32[]{:S(2)}) %copy-start.2) | copy-done | bytes 32792
  4.2 0.0 copy-start.3
  4.2 0.8 %copy-done.3 = bf16[1,128,128]{2,1,0:T(8,128)(2,1)S(1)} copy-done((bf16[1,128,128]{2,1,0:T(8,128)(2,1)S(1)}, bf16[1,128,128]{2,1,0:T(8,128)(2,1)}, u32[]{:S(2)}) %copy-start.3) | copy-done | bytes 32792
  5.0 0.0 copy-start.4
  5.0 0.8 %copy-done.4 = bf16[1,128,128]{2,1,0:T(8,128)(2,1)S(1)} copy-done((bf16[1,128,128]{2,1,0:T(8,128)(2,1)S(1)}, bf16[1,128,128]{2,1,0:T(8,128)(2,1)}, u32[]{:S(2)}) %copy-start.4) | copy-done | bytes 32792
  5.7 0.0 copy-start.5
  5.7 0.7 copy-done.5
  6.4 63.5 %attention_backward.1 = (f32[25,128]{1,0:T(8,128)S(1)}, bf16[1,128,384]{2,1,0:T(8,128)(2,1)S(1)}) custom-call(bf16[1,128,128]{2,1,0:T(8,128)(2,1)S(1)} %copy-done.2, bf16[1,128,128]{2,1,0:T(8,128)(2,1)S(1)} %copy-done.3, bf16[1,128,128]{2,1,0:T(8,128)(2,1)S(1)} %copy-done.4, bf16[1,128,12288]{2,1,0:T(8,128)(2,1)S(1)} %copy-done, ...), custom_call_target="tpu_custom_call" | custom-call | tf_op jit(solution)/shard_map/attention_backward/pallas_call | solution.py:378
  69.9 0.6 copy.10
  70.5 0.6 copy.11
Async XLA Ops:
  0.6 1.9 %copy-start = (bf16[1,128,12288]{2,1,0:T(8,128)(2,1)S(1)}, bf16[1,128,12288]{2,1,0:T(8,128)(2,1)}, u32[]{:S(2)}) copy-start(bf16[1,128,12288]{2,1,0:T(8,128)(2,1)} %o_hbm.1) | copy-start | bytes 9437188
  2.5 0.9 %copy-start.1 = (bf16[128,768]{1,0:T(8,128)(2,1)S(1)}, bf16[128,768]{1,0:T(8,128)(2,1)}, u32[]{:S(2)}) copy-start(bf16[128,768]{1,0:T(8,128)(2,1)} %w_hbm.1) | copy-start | bytes 589828
  3.4 0.8 %copy-start.2 = (bf16[1,128,128]{2,1,0:T(8,128)(2,1)S(1)}, bf16[1,128,128]{2,1,0:T(8,128)(2,1)}, u32[]{:S(2)}) copy-start(bf16[1,128,128]{2,1,0:T(8,128)(2,1)} %q_hbm.1) | copy-start | bytes 98308
  4.2 0.8 %copy-start.3 = (bf16[1,128,128]{2,1,0:T(8,128)(2,1)S(1)}, bf16[1,128,128]{2,1,0:T(8,128)(2,1)}, u32[]{:S(2)}) copy-start(bf16[1,128,128]{2,1,0:T(8,128)(2,1)} %k_hbm.1) | copy-start | bytes 98308
  5.0 0.8 %copy-start.4 = (bf16[1,128,128]{2,1,0:T(8,128)(2,1)S(1)}, bf16[1,128,128]{2,1,0:T(8,128)(2,1)}, u32[]{:S(2)}) copy-start(bf16[1,128,128]{2,1,0:T(8,128)(2,1)} %v_hbm.1) | copy-start | bytes 98308
  5.7 0.7 copy-start.5

commit v2 on v1

--- a/solution.py
+++ b/solution.py
@@ -19,7 +19,8 @@
 NB = 80
 B0 = 56
 PAD = 56
-GROWS = PAD + NB * PER + PAD
+STEP = 97
+GROWS = PAD + NB * STEP + PAD
 WIN = 50
 CHUNK = 400
 HALVES = ((0, 208), (208, 192))
@@ -33,8 +34,8 @@
     return lax.dot_general(a, b, (((ca,), (cb,)), ((), ())), preferred_element_type=F32)
 
 
-def kernel(q_hbm, k_hbm, v_hbm, o_hbm, w_hbm, off, bucket, qkv,
-           O, W, G, F, S, R, At, q, K, V, probs, hg, gsend, grecv, send2, recv2, tab,
+def kernel(q_hbm, k_hbm, v_hbm, o_hbm, w_hbm, off_hbm, bucket, qkv,
+           O, W, G, F, S, R, At, q, K, V, probs, hg, gsend, grecv, send2, recv2, off, tab,
            lsem, ssem, rsem, s2send, s2recv):
     node = lax.axis_index("node")
     group = lax.axis_index("group")
@@ -63,6 +64,14 @@
 
     sent = []
 
+    bar = pltpu.get_barrier_semaphore()
+    chip_line = [did(x + dx, y, z, dc) for dx in range(4) for dc in (k, 1 - k)][1:]
+    near = [prv, did(x, y + 1, z, k), did(x, y - 1, z, k), did(x, y, z + 1, k), did(x, y, z - 1, k)] + chip_line
+    for dev in near:
+        pl.semaphore_signal(bar, inc=1, device_id=dev, device_id_type=MESH)
+    src_core = x // 2
+    mine = src_core == k
+
     own_rows = pl.ds(pl.multiple_of(TOK * k, TOK), TOK)
     locals_ = [
         pltpu.make_async_copy(q_hbm.at[0], q, lsem.at[0]),
@@ -70,64 +79,15 @@
         pltpu.make_async_copy(v_hbm.at[0], V.at[pl.ds(TOK, TOK)], lsem.at[2]),
         pltpu.make_async_copy(o_hbm.at[0], O.at[own_rows], lsem.at[3]),
         pltpu.make_async_copy(w_hbm, W.at[node], lsem.at[4]),
+        pltpu.make_async_copy(off_hbm, off, lsem.at[5]),
     ]
     for c in locals_:
         c.start()
 
-    bar = pltpu.get_barrier_semaphore()
-
-    def sig(dev):
-        pl.semaphore_signal(bar, inc=1, device_id=dev, device_id_type=MESH)
-
-    near = [sib, nxt, prv, did(x, y + 1, z, k), did(x, y - 1, z, k), did(x, y, z + 1, k),
-            did(x, y, z - 1, k), did(x + 1, y, z, k), did(x - 1, y, z, k)]
-    for dev in near:
-        sig(dev)
-    src_core = x // 2
-    odd = lax.rem(x, 2)
-    mine = src_core == k
-
-    def sig_far(i, carry):
-        sx, r = i // 8, lax.rem(i, 8)
-        sy = jnp.where(odd == 1, r, y)
-        sz = jnp.where(odd == 1, z, r)
-
-        @pl.when(jnp.logical_not(mine & (sx == x) & (sy == y) & (sz == z)))
-        def _():
-            sig(did(sx, sy, sz, src_core))
-        return carry
-    lax.fori_loop(0, 32, sig_far, 0)
-
-    b0 = B0 * k
-
-    def off_row(i):
-        return lax.shift_right_logical(off[jnp.clip(i, 0, 128)], 7)
-
-    def advance(i, f0):
-        step = (i + 1 <= 128) & (off_row(i + 1) <= f0)
-        return i + step.astype(jnp.int32)
-
-    first = jnp.where(k == 0, -1, 61)
-    flat0 = 6400 * k
-    first = lax.fori_loop(0, 5, lambda _, i: advance(i, flat0), first)
-
-    def table(w, i):
-        f0 = flat0 + WIN * w
-        i = advance(i, f0)
-        a, b = off_row(i), off_row(i + 1)
-        one = PAD + (i - b0) * PER + jnp.clip(f0 - a, 0, PER)
-        two = PAD + (jnp.minimum(i + 1, 128) - b0) * PER + jnp.clip(f0 - b, -PAD, 0)
-        tab[0, w] = jnp.clip(one, 0, GROWS - 56)
-        tab[1, w] = jnp.clip(two, 0, GROWS - 56)
-        tab[2, w] = jnp.where(i < 0, 0, a + PER - f0)
-        tab[3, w] = jnp.where(i + 1 > 128, 2 * WIN, b - f0)
-        return i
-    lax.fori_loop(0, 128, table, first)
-
     rows8 = lax.broadcasted_iota(jnp.int32, (8, 2 * TOK), 0)
     At[pl.ds(HEAD, 8), :] = jnp.where(rows8 == 0, 1.0, 0.0)
 
-    pl.semaphore_wait(bar, len(near) + 32 - mine.astype(jnp.int32))
+    pl.semaphore_wait(bar, len(near))
 
     cp_k = send(k_hbm.at[0], K.at[pl.ds(0, TOK)], nxt)
     cp_v = send(v_hbm.at[0], V.at[pl.ds(0, TOK)], nxt)
@@ -155,7 +115,7 @@
     cp_o = [send(o_hbm.at[0, :, pl.ds(OW * j, OW)], O.at[own_rows, pl.ds(OW * j, OW)], sib)
             for j in range(OCH)]
 
-    f1, f2, wsib = {}, {}, []
+    f1, f2, wsib = {}, {}, {}
 
     def stage1(d):
         m1[d].wait_recv()
@@ -163,7 +123,7 @@
         f1[d] = send(wpart(n, 0 if d == 1 else 1), wpart(n, 0 if d == 1 else 1), nbr(0, d))
         for e in (1, -1):
             m2[-d, e] = send(wpart(n), wpart(n), nbr(1, e))
-        wsib.append(send(wpart(n), wpart(n), sib))
+        wsib[-d, 0] = send(wpart(n), wpart(n), sib)
 
     def stage1_far():
         for d in (1, -1):
@@ -171,7 +131,7 @@
         n = nid(2, 0)
         for e in (1, -1):
             m2[2, e] = send(wpart(n), wpart(n), nbr(1, e))
-        wsib.append(send(wpart(n), wpart(n), sib))
+        wsib[2, 0] = send(wpart(n), wpart(n), sib)
 
     def stage2(a):
         for e in (1, -1):
@@ -179,16 +139,40 @@
             n = nid(a, -e)
             sub = 0 if e == 1 else 1
             f2[a, e] = send(wpart(n, sub), wpart(n, sub), nbr(1, e))
-            wsib.append(send(wpart(n), wpart(n), sib))
+            wsib[a, -e] = send(wpart(n), wpart(n), sib)
 
     def stage2_far(a):
         for e in (1, -1):
             f2[a, e].wait_recv()
         n = nid(a, 2)
-        wsib.append(send(wpart(n), wpart(n), sib))
-
-    stage1(1)
-    stage1(-1)
+        wsib[a, 2] = send(wpart(n), wpart(n), sib)
+
+    b0 = B0 * k
+    locals_[5].wait()
+
+    def off_row(i):
+        return lax.shift_right_logical(off[jnp.clip(i, 0, 128)], 7)
+
+    def advance(i, f0):
+        step = (i + 1 <= 128) & (off_row(i + 1) <= f0)
+        return i + step.astype(jnp.int32)
+
+    first = jnp.where(k == 0, -1, 61)
+    flat0 = 6400 * k
+    first = lax.fori_loop(0, 5, lambda _, i: advance(i, flat0), first)
+
+    def table(w, i):
+        f0 = flat0 + WIN * w
+        i = advance(i, f0)
+        a, b = off_row(i), off_row(i + 1)
+        one = PAD + (i - b0) * STEP + jnp.clip(f0 - a, 0, PER)
+        two = PAD + (jnp.minimum(i + 1, 128) - b0) * STEP + jnp.clip(f0 - b, -PAD, 0)
+        tab[0, w] = jnp.clip(one, 0, GROWS - 56)
+        tab[1, w] = jnp.clip(two, 0, GROWS - 56)
+        tab[2, w] = jnp.where(i < 0, 0, a + PER - f0)
+        tab[3, w] = jnp.where(i + 1 > 128, 2 * WIN, b - f0)
+        return i
+    lax.fori_loop(0, 128, table, first)
 
     for c in locals_[:3]:
         c.wait()
@@ -210,21 +194,31 @@
     At[pl.ds(0, HEAD), att_cols] = jnp.transpose(att)
     cp_a = send(At.at[pl.ds(0, HEAD), att_cols], At.at[pl.ds(0, HEAD), att_cols], sib)
 
-    stage1_far()
-    stage2(0)
+    stage1(1)
+    stage1(-1)
 
     cp_a.wait_recv()
     locals_[3].wait()
     lhs = At[pl.ds(pl.multiple_of(b0, 8), NB), :].astype(BF)
-    for j in range(OCH):
+
+    def mul(t, carry):
+        prod = dot(lhs, O[:, pl.ds(pl.multiple_of(256 * t, 256), 256)], 1, 0)
+        G[pl.ds(PAD + 2 * t, NB, stride=STEP), :] = prod[:, :128]
+        G[pl.ds(PAD + 2 * t + 1, NB, stride=STEP), :] = prod[:, 128:]
+        return carry
+
+    def muls(j):
         cp_o[j].wait_recv()
-
-        def mul(t, carry):
-            prod = dot(lhs, O[:, pl.ds(pl.multiple_of(256 * t, 256), 256)], 1, 0)
-            G[pl.ds(PAD + 2 * t, NB, stride=PER), :] = prod[:, :128]
-            G[pl.ds(PAD + 2 * t + 1, NB, stride=PER), :] = prod[:, 128:]
-            return carry
-        lax.fori_loop(j * (OW // 256), (j + 1) * (OW // 256), mul, 0)
+        lax.fori_loop(j * (OW // 256), (j + 1) * (OW // 256), mul, 0, unroll=2)
+
+    muls(0)
+    muls(1)
+    stage1_far()
+    muls(2)
+    muls(3)
+    stage2(0)
+    muls(4)
+    muls(5)
 
     rwin = lax.broadcasted_iota(jnp.int32, (56, 128), 0)
 
@@ -266,33 +260,41 @@
     ring(3, 0)
     gather(-2)
     gather(2)
+    gather(-1)
+    gather(1)
+    gather(0)
+
+    hg[...] = jnp.zeros((TOK, HEAD), F32)
+    locals_[4].wait()
+
+    def head(keys, shards):
+        for key in keys:
+            wsib[key].wait_recv()
+        total = hg[...]
+        for dx, dz in shards:
+            n = lax.rem(x + dx + 4, 4) * 4 + lax.rem(zlo + dz + 4, 4)
+            cols = pl.ds(pl.multiple_of(COLS * n, COLS), COLS)
+            total = total + dot(O[own_rows, cols], W[n], 1, 1)
+        hg[...] = total
+
+    head([(1, 0), (-1, 0), (0, 1), (0, -1)], [(0, 0), (1, 0), (-1, 0), (0, 1), (0, -1)])
+    stage2(-1)
+    stage2(1)
     for ch in range(4):
         ring(ch, 1)
-    stage2(-1)
-    stage2(1)
+    head([(1, 1), (-1, 1), (1, -1), (-1, -1)], [(1, 1), (-1, 1), (1, -1), (-1, -1)])
     stage2_far(0)
-    gather(-1)
-    gather(1)
+    stage2(2)
     for ch in range(4):
         ring(ch, 2)
-    gather(0)
-    stage2(2)
     stage2_far(-1)
     stage2_far(1)
+    head([(2, 0), (0, 2)], [(2, 0), (0, 2)])
+    stage2_far(2)
     for ch in range(2):
         ring(ch, 3)
-    stage2_far(2)
-
-    locals_[4].wait()
-    for c in wsib:
-        c.wait_recv()
-    hg[...] = jnp.zeros((TOK, HEAD), F32)
-
-    def head(n, carry):
-        cols = pl.ds(pl.multiple_of(COLS * n, COLS), COLS)
-        hg[...] += dot(O[own_rows, cols], W[n], 1, 1)
-        return carry
-    lax.fori_loop(0, 16, head, 0)
+    head([(2, 1), (2, -1), (-1, 2), (1, 2), (2, 2)], [(2, 1), (2, -1), (1, 2), (-1, 2), (2, 2)])
+
     head_low = hg[...].astype(BF)
     prob_grad = dot(head_low, V[...], 1, 1)
     pr = probs[...]
@@ -308,7 +310,6 @@
     hg[...] = kg[TOK:]
     probs[:, pl.ds(0, HEAD)] = vg[TOK:]
 
-    last = {0: (0, 3), 1: (3, 2), 2: (2, 2), 3: (1, 3)}
     for a, p in ((0, y), (1, z)):
         for h, (lo, size) in enumerate(HALVES):
             total = S[a, p, pl.ds(lo, size)].astype(F32)
@@ -320,6 +321,7 @@
         for i in range(16):
             send2[16 * a + i] = F[a, pl.ds(25 * i, 32), :].astype(BF)
 
+    for a in range(2):
         def scatter(i, carry):
             r, dc = i // 2, lax.rem(i, 2)
             dx = 2 * k + a
@@ -372,13 +374,13 @@
 
 
 def per_device(queries, keys, values, out_grad, out_weight, block_offsets):
-    hbm = pl.BlockSpec(memory_space=pl.ANY)
+    hbm = pl.BlockSpec(memory_space=pltpu.HBM)
     vmem = pl.BlockSpec(memory_space=pltpu.VMEM)
     messages = 96
     bucket, qkv = pl.pallas_call(
         kernel,
         out_shape=(jax.ShapeDtypeStruct((25, 128), F32), jax.ShapeDtypeStruct((1, TOK, 3 * HEAD), BF)),
-        in_specs=[hbm] * 5 + [pl.BlockSpec(memory_space=pltpu.SMEM)],
+        in_specs=[hbm] * 6,
         out_specs=(vmem, vmem),
         scratch_shapes=[
             pltpu.VMEM((2 * TOK, WIDTH), BF),
@@ -397,15 +399,16 @@
             pltpu.VMEM((2 * TOK, HEAD), BF),
             pltpu.VMEM((32, 32, 128), BF),
             pltpu.VMEM((32, 32, 128), BF),
+            pltpu.SMEM((129,), jnp.int32),
             pltpu.SMEM((4, 128), jnp.int32),
-            pltpu.SemaphoreType.DMA((5,)),
+            pltpu.SemaphoreType.DMA((6,)),
             pltpu.SemaphoreType.DMA((messages,)),
             pltpu.SemaphoreType.DMA((messages,)),
             pltpu.SemaphoreType.DMA,
             pltpu.SemaphoreType.DMA,
         ],
         compiler_params=pltpu.CompilerParams(
-            collective_id=0, has_side_effects=True, vmem_limit_bytes=40 << 20),
+            collective_id=0, has_side_effects=True, vmem_limit_bytes=60 << 20),
         name="attention_backward",
     )(queries, keys, values, out_grad, out_weight, block_offsets)
     return bucket.reshape(3200), qkv

time: 71.8 us -> 55.2 us (0.77)
  Pallas kernels: 63.5 us -> 51.4 us
  local copies, waits for them, and re-layouts: 7.01 us -> 2.87 us
    pallas_call x1, Pallas kernels: 63.5 us -> 51.4 us  [per_device(): pl.pallas_call(kernel, out_shape=(jax.ShapeDtypeStruct((25, 128), F32), j...]
    unnamed x14 -> x2, local copies, waits for them, and re-layouts: 7.01 us -> 2.87 us
where the time goes in v2:
time: 55.2 us; the launch traced here: 54.9 us
  Pallas kernels  51.4 us (93%)
  local copies, waits for them, and re-layouts  2.87 us (5%)
  between operations  0.64 us (1%)
    pallas_call x1, Pallas kernels, per_device(): pl.pallas_call(kernel, out_shape=(jax.ShapeDtypeStruct((25, 128), F32), j...  51.4 us
    unnamed x2, local copies, waits for them, and re-layouts  2.87 us

profile of v2, /device:TPU:1, one launch (start us, length us, event | category | flops | bytes accessed | tf_op | source)
XLA Modules:
  0.0 54.9 jit_solution(8922454437491826878)
XLA Ops:
  0.6 51.4 %attention_backward.1 = (f32[25,128]{1,0:T(8,128)}, bf16[1,128,384]{2,1,0:T(8,128)(2,1)}) custom-call(bf16[1,128,128]{2,1,0:T(8,128)(2,1)} %q_hbm.1, bf16[1,128,128]{2,1,0:T(8,128)(2,1)} %k_hbm.1, bf16[1,128,128]{2,1,0:T(8,128)(2,1)} %v_hbm.1, bf16[1,128,12288]{2,1,0:T(8,128)(2,1)} %o_hbm.1, bf16[128,768]{1,0:T(8,128)(2,1)} %w_hbm.1, s32[129]{0:T(256)} %off_hbm.1), custom_call_target="tpu_custom_call" | custom-call | tf_op jit(solution)/shard_map/attention_backward/pallas_call | solution.py:380
  52.0 1.3 %copy.10 = f32[3200]{0:T(1024)} copy(f32[3200]{0:T(1024)} %bitcast.1) | data formatting | bytes 25600
  53.3 1.5 %copy.11 = bf16[1,128,384]{2,1,0:T(8,128)(2,1)} copy(bf16[1,128,384]{2,1,0:T(8,128)(2,1)} %get-tuple-element.9) | data formatting | bytes 196608

commit v3 on v2

v3 whole, which is shorter than its diff:
```python
import math

import jax
import jax.numpy as jnp
from jax import lax
from jax.experimental import pallas as pl
from jax.experimental.pallas import tpu as pltpu
from jax.sharding import PartitionSpec as P

MESH = pl.DeviceIdType.MESH
BF = jnp.bfloat16
F32 = jnp.float32

HEAD = 128
TOK = 128
WIDTH = 12288
COLS = 768
PER = 96
NB = 80
B0 = 56
PAD = 56
STEP = 97
GROWS = PAD + NB * STEP + PAD
WIN = 50
CHUNK = 400
HALVES = ((0, 208), (208, 192))
OCH = 6
OW = WIDTH // OCH

STEPS = ((-4, -2), (-3, -1), (3, 1), (-1, -1), (1, 1), (-2, -2), (2, 2))


def dot(a, b, ca, cb):
    return lax.dot_general(a, b, (((ca,), (cb,)), ((), ())), preferred_element_type=F32)


def kernel(q_hbm, k_hbm, v_hbm, o_hbm, w_hbm, off_hbm, bucket, qkv,
           O, W, G, F, S, R, At, q, K, V, probs, hg, gsend, grecv, send2, recv2, off, first, tab,
           lsem, ssem, rsem, s2send, s2recv):
    node = lax.axis_index("node")
    group = lax.axis_index("group")
    x, zlo = node // 4, node % 4
    y, zhi, k = group // 4, (group % 4) // 2, group % 2
    z = zhi * 4 + zlo

    def did(dx, dy, dz, dc):
        dx, dy, dz = (dx + 8) & 3, (dy + 16) & 7, (dz + 16) & 7
        return (dx * 4 + (dz & 3), dy * 4 + (dz >> 2) * 2 + dc)

    sib = did(x, y, z, 1 - k)
    nxt = (lax.rem(node + 1, 16), group)
    prv = (lax.rem(node + 15, 16), group)
    counter = [0]

    def send(src, dst, dev):
        i = counter[0]
        counter[0] += 1
        cp = pltpu.make_async_remote_copy(
            src_ref=src, dst_ref=dst, send_sem=ssem.at[i], recv_sem=rsem.at[i],
            device_id=dev, device_id_type=MESH)
        cp.start()
        sent.append(cp)
        return cp

    sent = []

    bar = pltpu.get_barrier_semaphore()
    chip_line = [did(x + dx, y, z, dc) for dx in range(4) for dc in (k, 1 - k)][1:]
    near = [prv] + [did(x, y + d, z, k) for d in (1, -1, 2, -2)] + [did(x, y, z + d, k) for d in (1, -1, 2, -2)] + chip_line
    for dev in near:
        pl.semaphore_signal(bar, inc=1, device_id=dev, device_id_type=MESH)
    src_core = x // 2
    mine = src_core == k

    own_rows = pl.ds(pl.multiple_of(TOK * k, TOK), TOK)
    locals_ = [
        pltpu.make_async_copy(q_hbm.at[0], q, lsem.at[0]),
        pltpu.make_async_copy(k_hbm.at[0], K.at[pl.ds(TOK, TOK)], lsem.at[1]),
        pltpu.make_async_copy(v_hbm.at[0], V.at[pl.ds(TOK, TOK)], lsem.at[2]),
        pltpu.make_async_copy(o_hbm.at[0], O.at[own_rows], lsem.at[3]),
        pltpu.make_async_copy(w_hbm, W.at[node], lsem.at[4]),
        pltpu.make_async_copy(off_hbm, off, lsem.at[5]),
    ]
    for c in locals_:
        c.start()

    rows8 = lax.broadcasted_iota(jnp.int32, (8, 2 * TOK), 0)
    At[pl.ds(HEAD, 8), :] = jnp.where(rows8 == 0, 1.0, 0.0)

    pl.semaphore_wait(bar, len(near))

    cp_k = send(k_hbm.at[0], K.at[pl.ds(0, TOK)], nxt)
    cp_v = send(v_hbm.at[0], V.at[pl.ds(0, TOK)], nxt)

    half = pl.multiple_of(64 * k, 64)

    def nbr(axis, delta):
        along_z = (k == 0) if axis == 0 else (k == 1)
        return did(x + jnp.where(along_z, 0, delta), y, z + jnp.where(along_z, delta, 0), k)

    def nid(a, b):
        dx, dz = jnp.where(k == 0, b, a), jnp.where(k == 0, a, b)
        return lax.rem(x + dx + 4, 4) * 4 + lax.rem(zlo + dz + 4, 4)

    def wpart(n):
        return W.at[n, pl.ds(half, 64)]

    def relay(n, e):
        part = W.at[n, pl.ds(half + (0 if e == 1 else 32), 32)]
        return send(part, part, nbr(relay_axis[0], e))

    relay_axis = [0]

    def spread(a, src):
        for e in (1, -1):
            m2[a, e] = send(src, wpart(nid(a, 0)), nbr(1, e))

    def share(a, b):
        wsib[a, b] = send(wpart(nid(a, b)), wpart(nid(a, b)), sib)

    def first_near():
        relay_axis[0] = 0
        for e in (1, -1):
            m1[e].wait_recv()
            f1[e] = relay(nid(-e, 0), e)
        for a in (-1, 1):
            spread(a, wpart(nid(a, 0)))
            share(a, 0)

    def first_far():
        for e in (1, -1):
            f1[e].wait_recv()
        spread(2, wpart(nid(2, 0)))
        share(2, 0)

    def second_near(a):
        relay_axis[0] = 1
        for e in (1, -1):
            m2[a, e].wait_recv()
            f2[a, e] = relay(nid(a, -e), e)
        for b in (-1, 1):
            share(a, b)

    def second_far(a):
        for e in (1, -1):
            f2[a, e].wait_recv()
        share(a, 2)

    w_own = w_hbm.at[pl.ds(half, 64)]
    m1, m2, f1, f2, wsib = {}, {}, {}, {}, {}
    for e in (1, -1):
        m1[e] = send(w_own, wpart(node), nbr(0, e))
    spread(0, w_own)
    cp_o = [send(o_hbm.at[0, :, pl.ds(OW * j, OW)], O.at[own_rows, pl.ds(OW * j, OW)], sib)
            for j in range(OCH)]

    b0 = B0 * k
    locals_[5].wait()
    for i in range(8):
        first[i] = -100000
        first[137 + i] = 100000

    def rows_of(i, carry):
        first[8 + i] = lax.shift_right_logical(off[i], 7)
        return carry
    lax.fori_loop(0, 129, rows_of, 0, unroll=43)

    def table(w):
        f0 = 6400 * k + WIN * w
        low = lax.shift_right_logical((f0 - 416 + 8 * PER) * 43691, 22)
        at = low
        for j in range(1, 6):
            at = at + (first[low + j] <= f0).astype(jnp.int32)
        a, b = first[at] - f0, first[at + 1] - f0
        base = PAD + (at - 8 - b0) * STEP
        tab[0, w] = base + jnp.minimum(-a, PER)
        tab[1, w] = base + STEP - jnp.clip(b, 0, PAD)
        tab[2, w] = a + PER
        tab[3, w] = b

    for c in locals_[:3]:
        c.wait()
    cp_k.wait_recv()
    cp_v.wait_recv()
    scale = 1.0 / math.sqrt(HEAD)
    scores = dot(q[...], K[...], 1, 1) * scale
    rp = lax.broadcasted_iota(jnp.int32, (TOK, 2 * TOK), 0)
    cpos = lax.broadcasted_iota(jnp.int32, (TOK, 2 * TOK), 1)
    lowest = jnp.where(node == 0, TOK, 0)
    allowed = (cpos > rp) & (cpos <= rp + TOK) & (cpos >= lowest)
    scores = jnp.where(allowed, scores, -jnp.inf)
    top = jnp.max(scores, axis=1, keepdims=True)
    expo = jnp.exp(scores - top)
    pr = expo / jnp.sum(expo, axis=1, keepdims=True)
    probs[...] = pr
    att = dot(pr.astype(BF), V[...], 1, 0)
    att_cols = pl.ds(pl.multiple_of(TOK * k, TOK), TOK)
    At[pl.ds(0, HEAD), att_cols] = jnp.transpose(att)
    cp_a = send(At.at[pl.ds(0, HEAD), att_cols], At.at[pl.ds(0, HEAD), att_cols], sib)
    first_near()

    cp_a.wait_recv()
    locals_[3].wait()
    lhs = At[pl.ds(pl.multiple_of(b0, 8), NB), :].astype(BF)

    for t in range(WIDTH // 256):
        if t % (OW // 256) == 0:
            cp_o[t // (OW // 256)].wait_recv()
        prod = dot(lhs, O[:, pl.ds(256 * t, 256)], 1, 0)
        G[pl.ds(PAD + 2 * t, NB, stride=STEP), :] = prod[:, :128]
        G[pl.ds(PAD + 2 * t + 1, NB, stride=STEP), :] = prod[:, 128:]
        for w in range(128 * t // 48, 128 * (t + 1) // 48):
            table(w)

    rwin = lax.broadcasted_iota(jnp.int32, (56, 128), 0)

    def gather(delta):
        for a, p in ((0, y), (1, z)):
            d = (p + delta + 16) & 7
            for m in range(8):
                if a == 0:
                    w = 16 * (m % 4) + 2 * d + m // 4
                else:
                    w = 64 + 16 * (d & 3) + 2 * m + (d >> 2)
                one = G[pl.ds(tab[0, w], 56), :]
                two = G[pl.ds(tab[1, w], 56), :]
                F[a, pl.ds(WIN * m, 56), :] = jnp.where(
                    rwin < tab[2, w], one, jnp.where(rwin >= tab[3, w], two, 0.0))
            S[a, d] = F[a, pl.ds(0, CHUNK), :].astype(BF)

    msgs = {}

    def ring(h, m, parts=()):
        lo, size = HALVES[h]
        sign = 1 - 2 * h
        owner, target = STEPS[m]
        rows = pl.ds(lo, size)
        for a, p in ((0, y), (1, z)):
            d = (p + sign * owner + 16) & 7
            if parts:
                total = S[a, d, rows].astype(F32)
                for i in parts:
                    msgs[a, h, i].wait_recv()
                    total = total + R[a, h, i, pl.ds(0, size)].astype(F32)
                S[a, d, rows] = total.astype(BF)
            t = sign * target
            to = did(x, y + t, z, k) if a == 0 else did(x, y, z + t, k)
            msgs[a, h, m] = send(S.at[a, d, rows], R.at[a, h, m, pl.ds(0, size)], to)

    for delta in (4, -3, 3):
        gather(delta)
    for m in (0, 1, 2):
        ring(0, m)
    for delta in (-1, 1, -2, 2, 0):
        gather(delta)
    for m in (0, 1, 2):
        ring(1, m)
    second_near(0)
    first_far()
    for m in (3, 4):
        ring(0, m)
        ring(1, m)
    second_near(-1)
    second_near(1)
    hg[...] = jnp.zeros((TOK, HEAD), F32)
    locals_[4].wait()

    def head(keys, shards):
        for key in keys:
            wsib[key].wait_recv()
        total = hg[...]
        for dx, dz in shards:
            n = ((x + dx + 4) & 3) * 4 + ((zlo + dz + 4) & 3)
            cols = pl.ds(pl.multiple_of(COLS * n, COLS), COLS)
            total = total + dot(O[own_rows, cols], W[n], 1, 1)
        hg[...] = total

    for h in (0, 1):
        ring(h, 5, (0, 1))
        ring(h, 6, (2,))
    second_near(2)
    second_far(0)
    head([(1, 0), (-1, 0), (2, 0), (0, 1), (0, -1), (0, 2)],
         [(0, 0), (1, 0), (-1, 0), (2, 0), (0, 1), (0, -1), (0, 2)])
    head([(1, 1), (-1, 1), (1, -1), (-1, -1)], [(1, 1), (-1, 1), (1, -1), (-1, -1)])
    second_far(-1)
    second_far(1)

    for h, (lo, size) in enumerate(HALVES):
        for a, p in ((0, y), (1, z)):
            total = S[a, p, pl.ds(lo, size)].astype(F32)
            for i in (3, 4, 5, 6):
                msgs[a, h, i].wait_recv()
                total = total + R[a, h, i, pl.ds(0, size)].astype(F32)
            F[a, pl.ds(lo, size), :] = total
            for i in range(8 * h, 8 * h + 8):
                send2[16 * a + i] = F[a, pl.ds(25 * i, 32), :].astype(BF)
        for i in range(8 * h, 8 * h + 8):
            r, dc = i // 2, i % 2
            for a, p in ((0, z), (1, y)):
                src, dst = send2.at[16 * a + i], recv2.at[x * 8 + p]
                to = did(2 * k + a, y, r, dc) if a == 0 else did(2 * k + a, r, z, dc)
                here = (2 * k + a == x) & (p == r) & (k == dc)

                @pl.when(jnp.logical_not(here))
                def _():
                    pltpu.make_async_remote_copy(
                        src_ref=src, dst_ref=dst, send_sem=s2send, recv_sem=s2recv,
                        device_id=to, device_id_type=MESH).start()

                @pl.when(here)
                def _():
                    pltpu.make_async_copy(src, dst, s2recv).start()

    second_far(2)
    head([(2, 1), (2, -1), (-1, 2), (1, 2), (2, 2)], [(2, 1), (2, -1), (1, 2), (-1, 2), (2, 2)])

    head_low = hg[...].astype(BF)
    prob_grad = dot(head_low, V[...], 1, 1)
    pr = probs[...]
    center = jnp.sum(pr * prob_grad, axis=1, keepdims=True)
    sg = pr * (prob_grad - center) * scale
    grad_q = dot(sg.astype(BF), K[...], 1, 0)
    kg = dot(jnp.transpose(sg).astype(BF), q[...], 1, 0)
    vg = dot(jnp.transpose(pr).astype(BF), head_low, 1, 0)
    gsend[pl.ds(0, TOK), :] = kg[:TOK].astype(BF)
    gsend[pl.ds(TOK, TOK), :] = vg[:TOK].astype(BF)
    cp_g = send(gsend, grecv, prv)
    qkv[0, :, pl.ds(0, HEAD)] = grad_q.astype(BF)
    hg[...] = kg[TOK:]
    probs[:, pl.ds(0, HEAD)] = vg[TOK:]


    cp_g.wait_recv()
    qkv[0, :, pl.ds(HEAD, HEAD)] = (hg[...] + grecv[pl.ds(0, TOK), :].astype(F32)).astype(BF)
    qkv[0, :, pl.ds(2 * HEAD, HEAD)] = (
        probs[:, pl.ds(0, HEAD)] + grecv[pl.ds(TOK, TOK), :].astype(F32)).astype(BF)

    pltpu.make_async_remote_copy(
        src_ref=send2, dst_ref=recv2, send_sem=s2send, recv_sem=s2recv,
        device_id=sib, device_id_type=MESH).wait_recv()
    acc = recv2[0].astype(F32)
    for s in range(1, 32):
        acc = acc + recv2[s].astype(F32)
    bucket[...] = acc[:25] * (1.0 / math.sqrt(65536))

    for c in sent:
        c.wait_send()

    def drain(count):
        pltpu.make_async_remote_copy(
            src_ref=send2.at[pl.ds(0, count)], dst_ref=recv2.at[pl.ds(0, count)],
            send_sem=s2send, recv_sem=s2recv, device_id=sib, device_id_type=MESH).wait_send()

    @pl.when(mine)
    def _():
        drain(31)

    @pl.when(jnp.logical_not(mine))
    def _():
        drain(32)


def per_device(queries, keys, values, out_grad, out_weight, block_offsets):
    hbm = pl.BlockSpec(memory_space=pltpu.HBM)
    vmem = pl.BlockSpec(memory_space=pltpu.VMEM)
    messages = 96
    bucket, qkv = pl.pallas_call(
        kernel,
        out_shape=(pltpu.VMEM((25, 128), F32), pltpu.VMEM((1, TOK, 3 * HEAD), BF)),
        in_specs=[hbm] * 6,
        out_specs=(vmem, vmem),
        scratch_shapes=[
            pltpu.VMEM((2 * TOK, WIDTH), BF),
            pltpu.VMEM((16, HEAD, COLS), BF),
            pltpu.VMEM((GROWS, 128), F32),
            pltpu.VMEM((2, 408, 128), F32),
            pltpu.VMEM((2, 8, CHUNK, 128), BF),
            pltpu.VMEM((2, 2, 7, 208, 128), BF),
            pltpu.VMEM((HEAD + 8, 2 * TOK), F32),
            pltpu.VMEM((TOK, HEAD), BF),
            pltpu.VMEM((2 * TOK, HEAD), BF),
            pltpu.VMEM((2 * TOK, HEAD), BF),
            pltpu.VMEM((TOK, 2 * TOK), F32),
            pltpu.VMEM((TOK, HEAD), F32),
            pltpu.VMEM((2 * TOK, HEAD), BF),
            pltpu.VMEM((2 * TOK, HEAD), BF),
            pltpu.VMEM((32, 32, 128), BF),
            pltpu.VMEM((32, 32, 128), BF),
            pltpu.SMEM((129,), jnp.int32),
            pltpu.SMEM((160,), jnp.int32),
            pltpu.SMEM((4, 128), jnp.int32),
            pltpu.SemaphoreType.DMA((6,)),
            pltpu.SemaphoreType.DMA((messages,)),
            pltpu.SemaphoreType.DMA((messages,)),
            pltpu.SemaphoreType.DMA,
            pltpu.SemaphoreType.DMA,
        ],
        compiler_params=pltpu.CompilerParams(
            collective_id=0, has_side_effects=True, vmem_limit_bytes=60 << 20),
        name="attention_backward",
    )(queries, keys, values, out_grad, out_weight, block_offsets)
    return bucket.reshape(3200), qkv


def solution(mesh):
    return jax.shard_map(
        per_device,
        mesh=mesh,
        in_specs=(
            P("group", "node", None),
            P("group", "node", None),
            P("group", "node", None),
            P("group", "node", None),
            P(None, "node"),
            P(),
        ),
        out_specs=(P(("node", "group")), P("group", "node", None)),
        check_vma=False,
    )
```

time: 55.2 us -> 48.2 us (0.87)
  the two profiles are of different devices: /device:TPU:1 before, /device:TPU:72 now
where the time goes in v3:
time: 48.2 us; the launch traced here: 48.1 us
  Pallas kernels  46.2 us (96%)
  local copies, waits for them, and re-layouts  1.25 us (3%)
  between operations  0.64 us (1%)
    pallas_call x1, Pallas kernels, per_device(): pl.pallas_call(kernel, out_shape=(pltpu.VMEM((25, 128), F32), pltpu.VMEM(...  46.2 us
    unnamed x2, local copies, waits for them, and re-layouts  1.25 us

profile of v3, /device:TPU:72, one launch (start us, length us, event | category | flops | bytes accessed | tf_op | source)
XLA Modules:
  0.0 48.1 jit_solution(16244349053383617637)
XLA Ops:
  0.6 46.2 %attention_backward.1 = (f32[25,128]{1,0:T(8,128)S(1)}, bf16[1,128,384]{2,1,0:T(8,128)(2,1)S(1)}) custom-call(bf16[1,128,128]{2,1,0:T(8,128)(2,1)} %q_hbm.1, bf16[1,128,128]{2,1,0:T(8,128)(2,1)} %k_hbm.1, bf16[1,128,128]{2,1,0:T(8,128)(2,1)} %v_hbm.1, bf16[1,128,12288]{2,1,0:T(8,128)(2,1)} %o_hbm.1, bf16[128,768]{1,0:T(8,128)(2,1)} %w_hbm.1, s32[129]{0:T(256)} %off_hbm.1), custom_call_target="tpu_custom_call" | custom-call | tf_op jit(solution)/shard_map/attention_backward/pallas_call | solution.py:368
  46.9 0.6 %copy.10 = f32[3200]{0:T(1024)} copy(f32[3200]{0:T(1024)S(1)} %bitcast.1) | data formatting | bytes 25600
  47.5 0.6 %copy.11 = bf16[1,128,384]{2,1,0:T(8,128)(2,1)} copy(bf16[1,128,384]{2,1,0:T(8,128)(2,1)S(1)} %get-tuple-element.7) | data formatting | bytes 196608

commit v4 on v3

--- a/solution.py
+++ b/solution.py
@@ -23,7 +23,7 @@
 GROWS = PAD + NB * STEP + PAD
 WIN = 50
 CHUNK = 400
-HALVES = ((0, 208), (208, 192))
+PARTS = ((0, 112), (112, 96), (208, 96), (304, 96))
 OCH = 6
 OW = WIDTH // OCH
 
@@ -52,14 +52,17 @@
     prv = (lax.rem(node + 15, 16), group)
     counter = [0]
 
-    def send(src, dst, dev):
+    def send(src, dst, dev, only=None):
         i = counter[0]
         counter[0] += 1
         cp = pltpu.make_async_remote_copy(
             src_ref=src, dst_ref=dst, send_sem=ssem.at[i], recv_sem=rsem.at[i],
             device_id=dev, device_id_type=MESH)
-        cp.start()
-        sent.append(cp)
+        if only is None:
+            cp.start()
+        else:
+            pl.when(only)(cp.start)
+        sent.append((cp, only))
         return cp
 
     sent = []
@@ -87,20 +90,30 @@
     rows8 = lax.broadcasted_iota(jnp.int32, (8, 2 * TOK), 0)
     At[pl.ds(HEAD, 8), :] = jnp.where(rows8 == 0, 1.0, 0.0)
 
+    nothing = jnp.zeros((TOK, HEAD), BF)
+
+    @pl.when(node == 0)
+    def _():
+        K[pl.ds(0, TOK), :] = nothing
+        V[pl.ds(0, TOK), :] = nothing
+
+    @pl.when(node == 15)
+    def _():
+        grecv[pl.ds(0, TOK), :] = nothing
+        grecv[pl.ds(TOK, TOK), :] = nothing
+
     pl.semaphore_wait(bar, len(near))
 
-    cp_k = send(k_hbm.at[0], K.at[pl.ds(0, TOK)], nxt)
-    cp_v = send(v_hbm.at[0], V.at[pl.ds(0, TOK)], nxt)
+    cp_k = send(k_hbm.at[0], K.at[pl.ds(0, TOK)], nxt, node < 15)
+    cp_v = send(v_hbm.at[0], V.at[pl.ds(0, TOK)], nxt, node < 15)
 
     half = pl.multiple_of(64 * k, 64)
 
     def nbr(axis, delta):
-        along_z = (k == 0) if axis == 0 else (k == 1)
-        return did(x + jnp.where(along_z, 0, delta), y, z + jnp.where(along_z, delta, 0), k)
+        return did(x, y, z + delta, k) if axis == 0 else did(x + delta, y, z, k)
 
     def nid(a, b):
-        dx, dz = jnp.where(k == 0, b, a), jnp.where(k == 0, a, b)
-        return lax.rem(x + dx + 4, 4) * 4 + lax.rem(zlo + dz + 4, 4)
+        return ((x + b + 4) & 3) * 4 + ((zlo + a + 4) & 3)
 
     def wpart(n):
         return W.at[n, pl.ds(half, 64)]
@@ -148,9 +161,6 @@
 
     w_own = w_hbm.at[pl.ds(half, 64)]
     m1, m2, f1, f2, wsib = {}, {}, {}, {}, {}
-    for e in (1, -1):
-        m1[e] = send(w_own, wpart(node), nbr(0, e))
-    spread(0, w_own)
     cp_o = [send(o_hbm.at[0, :, pl.ds(OW * j, OW)], O.at[own_rows, pl.ds(OW * j, OW)], sib)
             for j in range(OCH)]
 
@@ -178,10 +188,19 @@
         tab[2, w] = a + PER
         tab[3, w] = b
 
+    for w in range(48):
+        table(w)
+    for e in (1, -1):
+        m1[e] = send(w_own, wpart(node), nbr(0, e))
+    spread(0, w_own)
+    for w in range(48, 128):
+        table(w)
     for c in locals_[:3]:
         c.wait()
-    cp_k.wait_recv()
-    cp_v.wait_recv()
+    @pl.when(node > 0)
+    def _():
+        cp_k.wait_recv()
+        cp_v.wait_recv()
     scale = 1.0 / math.sqrt(HEAD)
     scores = dot(q[...], K[...], 1, 1) * scale
     rp = lax.broadcasted_iota(jnp.int32, (TOK, 2 * TOK), 0)
@@ -209,8 +228,6 @@
         prod = dot(lhs, O[:, pl.ds(256 * t, 256)], 1, 0)
         G[pl.ds(PAD + 2 * t, NB, stride=STEP), :] = prod[:, :128]
         G[pl.ds(PAD + 2 * t + 1, NB, stride=STEP), :] = prod[:, 128:]
-        for w in range(128 * t // 48, 128 * (t + 1) // 48):
-            table(w)
 
     rwin = lax.broadcasted_iota(jnp.int32, (56, 128), 0)
 
@@ -231,8 +248,8 @@
     msgs = {}
 
     def ring(h, m, parts=()):
-        lo, size = HALVES[h]
-        sign = 1 - 2 * h
+        lo, size = PARTS[h]
+        sign = 1 - 2 * (h % 2)
         owner, target = STEPS[m]
         rows = pl.ds(lo, size)
         for a, p in ((0, y), (1, z)):
@@ -251,15 +268,17 @@
         gather(delta)
     for m in (0, 1, 2):
         ring(0, m)
+        ring(1, m)
     for delta in (-1, 1, -2, 2, 0):
         gather(delta)
     for m in (0, 1, 2):
-        ring(1, m)
+        ring(2, m)
+        ring(3, m)
     second_near(0)
+    for h in range(4):
+        ring(h, 3)
+        ring(h, 4)
     first_far()
-    for m in (3, 4):
-        ring(0, m)
-        ring(1, m)
     second_near(-1)
     second_near(1)
     hg[...] = jnp.zeros((TOK, HEAD), F32)
@@ -275,27 +294,26 @@
             total = total + dot(O[own_rows, cols], W[n], 1, 1)
         hg[...] = total
 
-    for h in (0, 1):
+    for h in range(4):
+        ring(h, 6, (2,))
         ring(h, 5, (0, 1))
-        ring(h, 6, (2,))
     second_near(2)
     second_far(0)
     head([(1, 0), (-1, 0), (2, 0), (0, 1), (0, -1), (0, 2)],
          [(0, 0), (1, 0), (-1, 0), (2, 0), (0, 1), (0, -1), (0, 2)])
     head([(1, 1), (-1, 1), (1, -1), (-1, -1)], [(1, 1), (-1, 1), (1, -1), (-1, -1)])
-    second_far(-1)
-    second_far(1)
-
-    for h, (lo, size) in enumerate(HALVES):
+    for a in (2, -1, 1):
+        second_far(a)
+    for h, (lo, size) in enumerate(PARTS):
         for a, p in ((0, y), (1, z)):
             total = S[a, p, pl.ds(lo, size)].astype(F32)
             for i in (3, 4, 5, 6):
                 msgs[a, h, i].wait_recv()
                 total = total + R[a, h, i, pl.ds(0, size)].astype(F32)
             F[a, pl.ds(lo, size), :] = total
-            for i in range(8 * h, 8 * h + 8):
+            for i in range(4 * h, 4 * h + 4):
                 send2[16 * a + i] = F[a, pl.ds(25 * i, 32), :].astype(BF)
-        for i in range(8 * h, 8 * h + 8):
+        for i in range(4 * h, 4 * h + 4):
             r, dc = i // 2, i % 2
             for a, p in ((0, z), (1, y)):
                 src, dst = send2.at[16 * a + i], recv2.at[x * 8 + p]
@@ -312,7 +330,6 @@
                 def _():
                     pltpu.make_async_copy(src, dst, s2recv).start()
 
-    second_far(2)
     head([(2, 1), (2, -1), (-1, 2), (1, 2), (2, 2)], [(2, 1), (2, -1), (1, 2), (-1, 2), (2, 2)])
 
     head_low = hg[...].astype(BF)
@@ -325,13 +342,13 @@
     vg = dot(jnp.transpose(pr).astype(BF), head_low, 1, 0)
     gsend[pl.ds(0, TOK), :] = kg[:TOK].astype(BF)
     gsend[pl.ds(TOK, TOK), :] = vg[:TOK].astype(BF)
-    cp_g = send(gsend, grecv, prv)
+    cp_g = send(gsend, grecv, prv, node > 0)
     qkv[0, :, pl.ds(0, HEAD)] = grad_q.astype(BF)
     hg[...] = kg[TOK:]
     probs[:, pl.ds(0, HEAD)] = vg[TOK:]
 
 
-    cp_g.wait_recv()
+    pl.when(node < 15)(cp_g.wait_recv)
     qkv[0, :, pl.ds(HEAD, HEAD)] = (hg[...] + grecv[pl.ds(0, TOK), :].astype(F32)).astype(BF)
     qkv[0, :, pl.ds(2 * HEAD, HEAD)] = (
         probs[:, pl.ds(0, HEAD)] + grecv[pl.ds(TOK, TOK), :].astype(F32)).astype(BF)
@@ -344,8 +361,11 @@
         acc = acc + recv2[s].astype(F32)
     bucket[...] = acc[:25] * (1.0 / math.sqrt(65536))
 
-    for c in sent:
-        c.wait_send()
+    for c, only in sent:
+        if only is None:
+            c.wait_send()
+        else:
+            pl.when(only)(c.wait_send)
 
     def drain(count):
         pltpu.make_async_remote_copy(
@@ -364,7 +384,7 @@
 def per_device(queries, keys, values, out_grad, out_weight, block_offsets):
     hbm = pl.BlockSpec(memory_space=pltpu.HBM)
     vmem = pl.BlockSpec(memory_space=pltpu.VMEM)
-    messages = 96
+    messages = 128
     bucket, qkv = pl.pallas_call(
         kernel,
         out_shape=(pltpu.VMEM((25, 128), F32), pltpu.VMEM((1, TOK, 3 * HEAD), BF)),
@@ -376,7 +396,7 @@
             pltpu.VMEM((GROWS, 128), F32),
             pltpu.VMEM((2, 408, 128), F32),
             pltpu.VMEM((2, 8, CHUNK, 128), BF),
-            pltpu.VMEM((2, 2, 7, 208, 128), BF),
+            pltpu.VMEM((2, 4, 7, 112, 128), BF),
             pltpu.VMEM((HEAD + 8, 2 * TOK), F32),
             pltpu.VMEM((TOK, HEAD), BF),
             pltpu.VMEM((2 * TOK, HEAD), BF),

time: 48.2 us -> 46.6 us (0.967)
  the two profiles are of different devices: /device:TPU:72 before, /device:TPU:1 now
where the time goes in v4:
time: 46.6 us; the launch traced here: 46.5 us
  Pallas kernels  44.6 us (96%)
  local copies, waits for them, and re-layouts  1.25 us (3%)
  between operations  0.64 us (1%)
    pallas_call x1, Pallas kernels, per_device(): pl.pallas_call(kernel, out_shape=(pltpu.VMEM((25, 128), F32), pltpu.VMEM(...  44.6 us
    unnamed x2, local copies, waits for them, and re-layouts  1.25 us

profile of v4, /device:TPU:1, one launch (start us, length us, event | category | flops | bytes accessed | tf_op | source)
XLA Modules:
  0.0 46.5 jit_solution(6215866708578809759)
XLA Ops:
  0.6 44.6 %attention_backward.1 = (f32[25,128]{1,0:T(8,128)S(1)}, bf16[1,128,384]{2,1,0:T(8,128)(2,1)S(1)}) custom-call(bf16[1,128,128]{2,1,0:T(8,128)(2,1)} %q_hbm.1, bf16[1,128,128]{2,1,0:T(8,128)(2,1)} %k_hbm.1, bf16[1,128,128]{2,1,0:T(8,128)(2,1)} %v_hbm.1, bf16[1,128,12288]{2,1,0:T(8,128)(2,1)} %o_hbm.1, bf16[128,768]{1,0:T(8,128)(2,1)} %w_hbm.1, s32[129]{0:T(256)} %off_hbm.1), custom_call_target="tpu_custom_call" | custom-call | tf_op jit(solution)/shard_map/attention_backward/pallas_call | solution.py:388
  45.2 0.6 %copy.10 = f32[3200]{0:T(1024)} copy(f32[3200]{0:T(1024)S(1)} %bitcast.1) | data formatting | bytes 25600
  45.8 0.6 %copy.11 = bf16[1,128,384]{2,1,0:T(8,128)(2,1)} copy(bf16[1,128,384]{2,1,0:T(8,128)(2,1)S(1)} %get-tuple-element.7) | data formatting | bytes 196608

commit v5 on v4

--- a/solution.py
+++ b/solution.py
@@ -275,9 +275,6 @@
         ring(2, m)
         ring(3, m)
     second_near(0)
-    for h in range(4):
-        ring(h, 3)
-        ring(h, 4)
     first_far()
     second_near(-1)
     second_near(1)
@@ -294,9 +291,18 @@
             total = total + dot(O[own_rows, cols], W[n], 1, 1)
         hg[...] = total
 
-    for h in range(4):
+    for h in (0, 1):
         ring(h, 6, (2,))
         ring(h, 5, (0, 1))
+    for h in (0, 1):
+        ring(h, 3)
+        ring(h, 4)
+    for h in (2, 3):
+        ring(h, 6, (2,))
+        ring(h, 5, (0, 1))
+    for h in (2, 3):
+        ring(h, 3)
+        ring(h, 4)
     second_near(2)
     second_far(0)
     head([(1, 0), (-1, 0), (2, 0), (0, 1), (0, -1), (0, 2)],

time: 46.6 us -> 46.2 us (level)
  the two profiles are of different devices: /device:TPU:1 before, /device:TPU:59 now
where the time goes in v5:
time: 46.2 us; the launch traced here: 46.1 us
  Pallas kernels  44.3 us (96%)
  local copies, waits for them, and re-layouts  1.25 us (3%)
  between operations  0.64 us (1%)
    pallas_call x1, Pallas kernels, per_device(): pl.pallas_call(kernel, out_shape=(pltpu.VMEM((25, 128), F32), pltpu.VMEM(...  44.3 us
    unnamed x2, local copies, waits for them, and re-layouts  1.25 us

profile of v5, /device:TPU:59, one launch (start us, length us, event | category | flops | bytes accessed | tf_op | source)
XLA Modules:
  0.0 46.1 jit_solution(5301729799432939523)
XLA Ops:
  0.6 44.3 %attention_backward.1 = (f32[25,128]{1,0:T(8,128)S(1)}, bf16[1,128,384]{2,1,0:T(8,128)(2,1)S(1)}) custom-call(bf16[1,128,128]{2,1,0:T(8,128)(2,1)} %q_hbm.1, bf16[1,128,128]{2,1,0:T(8,128)(2,1)} %k_hbm.1, bf16[1,128,128]{2,1,0:T(8,128)(2,1)} %v_hbm.1, bf16[1,128,12288]{2,1,0:T(8,128)(2,1)} %o_hbm.1, bf16[128,768]{1,0:T(8,128)(2,1)} %w_hbm.1, s32[129]{0:T(256)} %off_hbm.1), custom_call_target="tpu_custom_call" | custom-call | tf_op jit(solution)/shard_map/attention_backward/pallas_call | solution.py:394
  44.9 0.6 %copy.10 = f32[3200]{0:T(1024)} copy(f32[3200]{0:T(1024)S(1)} %bitcast.1) | data formatting | bytes 25600
  45.5 0.6 %copy.11 = bf16[1,128,384]{2,1,0:T(8,128)(2,1)} copy(bf16[1,128,384]{2,1,0:T(8,128)(2,1)S(1)} %get-tuple-element.7) | data formatting | bytes 196608
